TPU v7x, 32 devices: a whole 2x2x4 slice. The times are simulated.
32 devices in a mesh: row: 4 (over y, core), col: 8 (over z, x).
Axes of the slice: x: 2, y: 2, z: 4, core: 2. Of those that a mesh axis runs over, the one named last changes fastest.
Arguments:
- child_fronts: bfloat16 [128, 768, 768], P(('row', 'col')), as said below
- child_tiles: int32 [128, 2], P(('row', 'col')), may hold values from 0 to 7, as said below
- child_parent: int32 [128, 1], P(('row', 'col')), may hold values from 0 to 7; in each aligned block of 4 rows (0 to 3, 4 to 7, ...) at most 2 rows name the same one
- parent_front: float32 [8, 1024, 1024], P('col', 'row'), as said below
Outputs:
- child_lower: bfloat16 [128, 256, 512], P(('row', 'col'))
- parent_panel: float32 [8, 1024, 512], P('col', 'row')
- parent_rest: float32 [8, 1024, 512], P('col', 'row')
Inputs may be any that keep to these rules, and one draw needn't show every extreme that they name: `child_tiles`: each child's block tiles are distinct and increasing. `child_parent`: among the children of one device no parent is named more than 2 times, a bound that some block reaches. `child_fronts`: each child front is symmetric positive definite. `parent_front`: each parent front is symmetric positive definite.
All inputs are finite; a program needn't handle non-finite values.
Results may differ from a plain program's by a relative error of at most 0.001.
Values sent between devices are 32-bit elements; how exact they have to be, the bound alone decides.
A program may use at most 128 MiB of HBM per device.

v0:
```python
import jax
import jax.numpy as jnp
from jax import lax
from jax.sharding import PartitionSpec as P

S1 = 512
TILE = 128
RT1 = 2
PT = 8
PT2 = 4
CAP = 2


def spread(value, axis, source):
    kept = jnp.where(lax.axis_index(axis) == source, value, 0).astype(value.dtype)
    return lax.psum(kept, axis)


def factor_children(fronts):
    whole_fronts = fronts.astype(jnp.float32)
    pivot_blocks = whole_fronts[:, :S1, :S1]
    below_blocks = whole_fronts[:, S1:, :S1]
    corners = whole_fronts[:, S1:, S1:]
    lower_factors = jnp.linalg.cholesky(pivot_blocks)
    solved = jax.scipy.linalg.solve_triangular(
        lower_factors, jnp.swapaxes(below_blocks, 1, 2), lower=True
    )
    child_panels = jnp.swapaxes(solved, 1, 2)
    products = jnp.einsum(
        "krs,kqs->krq", child_panels, child_panels, precision=lax.Precision.HIGHEST
    )
    schur_blocks = corners - products
    return (child_panels.astype(jnp.bfloat16), schur_blocks)


def local(child_fronts, child_tiles, child_parent, parent_front):
    child_lower, schurs = factor_children(child_fronts)
    groups = lax.axis_size("col")
    kid_count = child_parent.shape[0]
    update_rows = schurs.shape[1]
    parent_ids = child_parent[:, 0]
    kid_order = jnp.arange(kid_count)
    earlier = (parent_ids[:, None] == parent_ids[None, :]) & (
        kid_order[None, :] < kid_order[:, None]
    )
    slot_index = jnp.sum(earlier.astype(jnp.int32), axis=1)
    target = parent_ids * CAP + slot_index
    outgoing_tiles = jnp.zeros((groups * CAP, RT1), jnp.int32).at[target].set(child_tiles)
    outgoing_tiles = outgoing_tiles.reshape(groups, CAP, RT1)
    outgoing = (
        jnp.zeros((groups * CAP, update_rows, update_rows), jnp.float32).at[target].set(schurs)
    )
    outgoing = outgoing.reshape(groups, CAP, update_rows, update_rows)
    received, received_tiles = (
        lax.all_to_all(outgoing, "col", split_axis=0, concat_axis=0, tiled=True),
        lax.all_to_all(outgoing_tiles, "col", split_axis=0, concat_axis=0, tiled=True),
    )
    received = received.reshape(groups * CAP, RT1, TILE, RT1, TILE)
    tile_blocks = received.transpose(0, 1, 3, 2, 4)
    received_tiles = received_tiles.reshape(groups * CAP, RT1)
    tile_grid = jnp.zeros((PT, PT, TILE, TILE), jnp.float32)
    tile_grid = tile_grid.at[received_tiles[:, :, None], received_tiles[:, None, :]].add(
        tile_blocks
    )
    summed_front = tile_grid.transpose(0, 2, 1, 3).reshape(PT * TILE, PT * TILE)
    height = parent_front.shape[1]
    added = lax.psum_scatter(summed_front, "row", scatter_dimension=0, tiled=True)
    front_rows = parent_front[0] + added
    my_index = lax.axis_index("row")
    first_row = my_index * height
    global_rows = first_row + jnp.arange(height)
    columns_out = []
    for panel_index in range(PT2):
        start_col = panel_index * TILE
        panel_block = front_rows[:, start_col : start_col + TILE]
        owner = start_col // height
        offset = jnp.clip(start_col - first_row, 0, height - TILE)
        local_diag = lax.dynamic_slice_in_dim(panel_block, offset, TILE, 0)
        guarded = jnp.where(my_index == owner, local_diag, jnp.eye(TILE, dtype=jnp.float32))
        diag_factor = spread(jnp.linalg.cholesky(guarded), "row", owner)
        own_rows = jax.scipy.linalg.solve_triangular(diag_factor, panel_block.T, lower=True).T
        own_rows = jnp.where((global_rows >= start_col)[:, None], own_rows, jnp.float32(0.0))
        column = lax.all_gather(own_rows, "row", axis=0, tiled=True)
        front_rows = front_rows - jnp.dot(own_rows, column.T, precision=lax.Precision.HIGHEST)
        columns_out.append(own_rows)
    parent_panel = jnp.concatenate(columns_out, axis=1)[None]
    split_col = PT2 * TILE
    parent_rest = jnp.where(
        (global_rows >= split_col)[:, None], front_rows[:, split_col:], jnp.float32(0.0)
    )[None]
    return (child_lower, parent_panel, parent_rest)


def solution(mesh):
    placed = (
        P(("row", "col"), None, None),
        P(("row", "col"), None),
        P(("row", "col"), None),
        P("col", "row", None),
    )
    return jax.shard_map(
        local,
        mesh=mesh,
        in_specs=placed,
        out_specs=(P(("row", "col"), None, None), P("col", "row", None), P("col", "row", None)),
        check_vma=False,
    )
```

profile of v0, /device:TPU:0, one launch (start us, length us, event | category | flops | bytes accessed | tf_op | source)
XLA Modules:
  0.0 1033.4 jit_solution(8389813515130258891)
XLA Ops:
  49.6 46.9 %custom-call.40 = f32[4,128,128]{2,1,0:T(8,128)S(1)} custom-call(f32[4,128,128]{2,1,0:T(8,128)S(1)} %cholesky.414), custom_call_target="Cholesky" | custom-call | tf_op jit(solution)/shard_map/jit(cholesky)/cholesky | solution.py:24
  99.0 39.3 %custom-call.41 = f32[4,1,128,128]{2,3,1,0:T(8,128)S(1)} custom-call(f32[4,1,128,128]{3,2,1,0:T(8,128)S(1)} %select_bitcast_fusion.2), custom_call_target="InvertDiagBlocksLowerTriangular" | custom-call | tf_op jit(solution)/shard_map/jit(cholesky)/cholesky | solution.py:24
  143.9 48.8 %custom-call.42 = f32[4,128,128]{2,1,0:T(8,128)} custom-call(f32[4,128,128]{2,1,0:T(8,128)} %cholesky.418), custom_call_target="Cholesky" | custom-call | tf_op jit(solution)/shard_map/jit(cholesky)/cholesky | solution.py:24
  194.5 40.7 %custom-call.43 = f32[4,1,128,128]{2,3,1,0:T(8,128)} custom-call(f32[4,1,128,128]{3,2,1,0:T(8,128)} %get-tuple-element.45), custom_call_target="InvertDiagBlocksLowerTriangular" | custom-call | tf_op jit(solution)/shard_map/jit(cholesky)/cholesky | solution.py:24
  241.0 48.3 %custom-call.44 = f32[4,128,128]{2,1,0:T(8,128)} custom-call(f32[4,128,128]{2,1,0:T(8,128)} %cholesky.423), custom_call_target="Cholesky" | custom-call | tf_op jit(solution)/shard_map/jit(cholesky)/cholesky | solution.py:24
  291.1 40.9 %custom-call.45 = f32[4,1,128,128]{2,3,1,0:T(8,128)} custom-call(f32[4,1,128,128]{3,2,1,0:T(8,128)} %get-tuple-element.43), custom_call_target="InvertDiagBlocksLowerTriangular" | custom-call | tf_op jit(solution)/shard_map/jit(cholesky)/cholesky | solution.py:24
  336.8 46.9 %custom-call.46 = f32[4,128,128]{2,1,0:T(8,128)S(1)} custom-call(f32[4,128,128]{2,1,0:T(8,128)S(1)} %convolution_subtract_fusion.8), custom_call_target="Cholesky" | custom-call | tf_op jit(solution)/shard_map/jit(cholesky)/cholesky | solution.py:24
  390.8 15.2 %while.1 = (s32[]{:T(128)}, f32[4,512,512]{2,1,0:T(8,128)}, s32[4,2]{0,1:T(2,128)S(1)}, f32[4,4,128,128]{3,2,0,1:T(8,128)}, s32[]{:T(128)}) while((s32[]{:T(128)}, f32[4,512,512]{2,1,0:T(8,128)}, s32[4,2]{0,1:T(2,128)S(1)}, f32[4,4,128,128]{3,2,0,1:T(8,128)}, s32[]{:T(128)}) %tuple.40), condition=%wide.while_cond, body=%wide.while_body.sunk | while | flops 2 | bytes 525421 | solution.py:25
  406.0 158.8 %custom-call.47 = f32[4,4,128,128]{2,3,1,0:T(8,128)} custom-call(f32[4,4,128,128]{3,2,1,0:T(8,128)} %bitcast.170), custom_call_target="InvertDiagBlocksLowerTriangular" | custom-call | tf_op jit(solution)/shard_map/jit(_solve_triangular)/vmap()/triangular_solve | solution.py:25
  592.8 92.3 %all-to-all-done.1 = f32[8,2,256,256]{3,2,1,0:T(8,128)} async-done(((f32[8,2,256,256]{3,2,1,0:T(8,128)}), f32[8,2,256,256]{3,2,1,0:T(8,128)}, u32[]{:S(2)}, u32[]{:S(2)}) %all-to-all-start.1) | async-done | bytes 4194336 | tf_op jit(solution)/shard_map/all_to_all | solution.py:55
  698.4 15.8 %scatter_fusion.1 = f32[8,8,128,128]{3,2,1,0:T(8,128)} fusion(f32[8,8,128,128]{3,2,1,0:T(8,128)} %broadcast_in_dim.89, s32[64]{0:T(128)S(1)} %reshape.182, f32[64,128,128]{2,1,0:T(8,128)} %bitcast.155), kind=kCustom, calls=%fused_computation.2 | custom fusion | flops 1048576 | bytes 12583424 | tf_op jit(solution)/shard_map/scatter-add | solution.py:62
  723.0 42.3 %reduce-scatter.2.cloned.1.call-done = f32[256,1024]{1,0:T(8,128)} async-done(((f32[1024,1024]{1,0:T(8,128)}), f32[256,1024]{1,0:T(8,128)}) %reduce-scatter.2.cloned.1.call-update) | async-done | bytes 1048592 | tf_op jit(solution)/shard_map/reduce_scatter | solution.py:67
  767.3 11.7 %cholesky.372 = f32[128,128]{1,0:T(8,128)S(1)} custom-call(f32[128,128]{1,0:T(8,128)S(1)} %copy.167), custom_call_target="Cholesky" | custom-call | tf_op jit(solution)/shard_map/jit(cholesky)/cholesky | solution.py:80
  781.2 31.0 %all-reduce.6.cloned.1.call-done = f32[128,128]{1,0:T(8,128)} async-done(((f32[128,128]{1,0:T(8,128)}), f32[128,128]{1,0:T(8,128)}) %all-reduce.6.cloned.1.call-update) | async-done | bytes 65552 | tf_op jit(solution)/shard_map/psum | solution.py:16
  813.1 9.8 custom-call.53
  831.0 11.7 %cholesky.383 = f32[128,128]{1,0:T(8,128)S(1)} custom-call(f32[128,128]{1,0:T(8,128)S(1)} %copy.169), custom_call_target="Cholesky" | custom-call | tf_op jit(solution)/shard_map/jit(cholesky)/cholesky | solution.py:80
  844.8 31.8 %all-reduce.8.cloned.1.call-done = f32[128,128]{1,0:T(8,128)} async-done(((f32[128,128]{1,0:T(8,128)}), f32[128,128]{1,0:T(8,128)}) %all-reduce.8.cloned.1.call-update) | async-done | bytes 65552 | tf_op jit(solution)/shard_map/psum | solution.py:16
  877.5 9.8 custom-call.54
  895.7 11.7 %cholesky.394 = f32[128,128]{1,0:T(8,128)S(1)} custom-call(f32[128,128]{1,0:T(8,128)S(1)} %copy.171), custom_call_target="Cholesky" | custom-call | tf_op jit(solution)/shard_map/jit(cholesky)/cholesky | solution.py:80
  909.4 31.8 %all-reduce.10.cloned.1.call-done = f32[128,128]{1,0:T(8,128)} async-done(((f32[128,128]{1,0:T(8,128)}), f32[128,128]{1,0:T(8,128)}) %all-reduce.10.cloned.1.call-update) | async-done | bytes 65552 | tf_op jit(solution)/shard_map/psum | solution.py:16
  942.1 9.8 custom-call.55
  960.3 11.7 %cholesky.405 = f32[128,128]{1,0:T(8,128)S(1)} custom-call(f32[128,128]{1,0:T(8,128)S(1)} %copy.173), custom_call_target="Cholesky" | custom-call | tf_op jit(solution)/shard_map/jit(cholesky)/cholesky | solution.py:80
  975.4 30.5 %all-reduce.12.cloned.1.call-done = f32[128,128]{1,0:T(8,128)} async-done(((f32[128,128]{1,0:T(8,128)}), f32[128,128]{1,0:T(8,128)}) %all-reduce.12.cloned.1.call-update) | async-done | bytes 65552 | tf_op jit(solution)/shard_map/psum | solution.py:16
  1006.8 9.8 custom-call.56
  (162 shorter events, 186.2 us)
Async XLA Ops:
  10.8 575.6 %all-to-all-start = ((s32[8,2,2]{1,2,0:T(2,128)}), s32[8,2,2]{1,2,0:T(2,128)S(1)}, u32[]{:S(2)}, u32[]{:S(2)}) async-start(s32[8,2,2]{1,2,0:T(2,128)} %copy.156), calls=%async_computation | async-start | bytes 16384 | tf_op jit(solution)/shard_map/all_to_all | solution.py:56
  24.7 6.8 slice-start
  27.2 4.4 slice-start.1
  41.4 2.8 copy-start
  47.5 2.1 copy-start.1
  237.6 146.1 %copy-start.7 = (f32[4,128,128]{2,1,0:T(8,128)S(1)}, f32[4,128,128]{2,1,0:T(8,128)}, u32[]{:S(2)}) copy-start(f32[4,128,128]{2,1,0:T(8,128)} %custom-call.42) | copy-start | bytes 786436
  564.8 6.5 copy-start.6
  572.0 3.2 copy-start.2
  575.2 0.8 copy-start.4
  586.4 98.7 %all-to-all-start.1 = ((f32[8,2,256,256]{3,2,1,0:T(8,128)}), f32[8,2,256,256]{3,2,1,0:T(8,128)}, u32[]{:S(2)}, u32[]{:S(2)}) async-start(f32[8,2,256,256]{3,2,1,0:T(8,128)} %bitcast.154), calls=%async_computation.1 | async-start | bytes 8388608 | tf_op jit(solution)/shard_map/all_to_all | solution.py:55
  592.3 173.0 %reduce-scatter.2.cloned.1.call-start = ((), (), s32[]{:S(2)}) async-start(), calls=%async_computation.3 | async-start | bytes 5242880 | tf_op jit(solution)/shard_map/reduce_scatter | solution.py:67
  721.7 1.0 copy-start.3
  721.7 1.2 copy-start.5
  721.7 90.5 %all-reduce.6.cloned.1.call-start = ((), (), s32[]{:S(2)}) async-start(), calls=%async_computation.4 | async-start | bytes 131072 | tf_op jit(solution)/shard_map/psum | solution.py:16
  781.0 95.6 %all-reduce.8.cloned.1.call-start = ((), (), s32[]{:S(2)}) async-start(), calls=%async_computation.5 | async-start | bytes 131072 | tf_op jit(solution)/shard_map/psum | solution.py:16
  844.7 96.5 %all-reduce.10.cloned.1.call-start = ((), (), s32[]{:S(2)}) async-start(), calls=%async_computation.6 | async-start | bytes 131072 | tf_op jit(solution)/shard_map/psum | solution.py:16
  909.4 96.5 %all-reduce.12.cloned.1.call-start = ((), (), s32[]{:S(2)}) async-start(), calls=%async_computation.7 | async-start | bytes 131072 | tf_op jit(solution)/shard_map/psum | solution.py:16
Sparse Core Ops, SparseCore 0:
  721.8 43.4 reduce-scatter.1
  781.1 31.0 all-reduce.5
  844.9 31.7 all-reduce.7
  909.5 31.7 all-reduce.9
  974.1 31.7 all-reduce.11
where the time goes:
time: 1040 us; the launch traced here: 1030 us
  other arithmetic  607 us (58%)
  waiting for transfers between devices  260 us (25%)
  local copies, waits for them, and re-layouts  76.4 us (7%)
  matrix products  35.2 us (3%)
  blocking collectives  26.5 us (3%)
  between operations  14.8 us (1%)
  starting transfers between devices  13.6 us (1%)
    another operation x16, other arithmetic, factor_children(): lower_factors = jnp.linalg.cholesky(pivot_blocks)  318 us
    another operation x4, other arithmetic, factor_children(): jax.scipy.linalg.solve_triangular(lower_factors, jnp.swapaxes(below_block...  164 us
    psum x4, waiting for transfers between devices, spread(): return lax.psum(kept, axis)  125 us
    all_to_all x1, waiting for transfers between devices, local(): lax.all_to_all(outgoing, 'col', split_axis=0, concat_axis=0, tiled=True)  92.3 us
    another operation x12, other arithmetic, local(): diag_factor = spread(jnp.linalg.cholesky(guarded), 'row', owner)  49.6 us
    another operation x8, other arithmetic, local(): jax.scipy.linalg.solve_triangular(diag_factor, panel_block.T, lower=True)  42.6 us
    reduce_scatter x1, waiting for transfers between devices, local(): lax.psum_scatter(summed_front, 'row', scatter_dimension=0, tiled=True)  42.3 us
    all_gather x4, blocking collectives, local(): column = lax.all_gather(own_rows, 'row', axis=0, tiled=True)  26.5 us
  transfers between devices with their start and end apart: 7, of which 6 were waited for; matrix products, arithmetic and copies ran while one was open for 55% of the time, Pallas kernels for 0%

commit v1 on v0

v1 whole, which is shorter than its diff:
```python
import functools
import jax
import jax.numpy as jnp
from jax import lax
from jax.experimental import pallas as pl
from jax.experimental.pallas import tpu as pltpu
from jax.sharding import PartitionSpec as P

S1 = 512
TILE = 128
RT1 = 2
PT = 8
PT2 = 4
CAP = 2
STRIP = 16
VMEM_BYTES = 56 * 1024 * 1024
F32 = jnp.float32


def split(x):
    hi = x.astype(jnp.bfloat16)
    lo = (x - hi.astype(F32)).astype(jnp.bfloat16)
    return hi, lo


def dot_nn(a, b):
    ah, al = split(a)
    bh, bl = split(b)
    return jnp.dot(
        jnp.concatenate([ah, ah, al], axis=1),
        jnp.concatenate([bh, bl, bh], axis=0),
        preferred_element_type=F32,
    )


def dot_tn(a, b):
    ah, al = split(a)
    bh, bl = split(b)
    return lax.dot_general(
        jnp.concatenate([ah, ah, al], axis=0),
        jnp.concatenate([bh, bl, bh], axis=0),
        (((0,), (0,)), ((), ())),
        preferred_element_type=F32,
    )


def factor_tiles(work, twin, kids):
    for first in range(0, TILE, STRIP):
        rows = [work[pl.ds(first + i, 2 * kids, stride=TILE), :] for i in range(STRIP)]
        heads = [twin[pl.ds(first + i, 2 * kids, stride=TILE), :] for i in range(STRIP)]
        coef = {}
        for i in range(STRIP):
            for k in range(i, STRIP):
                lane = heads[i][:, first + k : first + k + 1]
                coef[i, k] = jnp.broadcast_to(lane, (2 * kids, TILE))
        for j in range(STRIP):
            scale = lax.rsqrt(coef[j, j])
            line = {k: coef[j, k] * scale for k in range(j + 1, STRIP)}
            rows[j] = rows[j] * scale
            for i in range(j + 1, STRIP):
                for k in range(i, STRIP):
                    coef[i, k] = coef[i, k] - line[i] * line[k]
                rows[i] = rows[i] - line[i] * rows[j]
        for i in range(STRIP):
            work[pl.ds(first + i, 2 * kids, stride=TILE), :] = rows[i]
        after = first + STRIP
        if after == TILE:
            break
        for k in range(kids):
            upper = work[k * TILE + first : k * TILE + after, :]
            inverse = work[(kids + k) * TILE + first : (kids + k) * TILE + after, :]
            change = dot_tn(upper, jnp.concatenate([upper, inverse], axis=1))
            head = slice(k * TILE + after, (k + 1) * TILE)
            tail = slice((kids + k) * TILE + after, (kids + k + 1) * TILE)
            fresh = work[head, :] - change[after:, :TILE]
            work[head, :] = fresh
            twin[head, :] = fresh
            twin[tail, :] = fresh
            work[tail, :] = work[tail, :] - change[after:, TILE:]


def load_tile(work, twin, kids, k, tile):
    rows = pl.ds(k * TILE, TILE)
    mirror = pl.ds((kids + k) * TILE, TILE)
    work[rows, :] = tile
    twin[rows, :] = tile
    twin[mirror, :] = tile
    r = lax.broadcasted_iota(jnp.int32, (TILE, TILE), 0)
    c = lax.broadcasted_iota(jnp.int32, (TILE, TILE), 1)
    work[mirror, :] = jnp.where(r == c, 1.0, 0.0).astype(F32)


def child_kernel(target, fronts, lower, outgoing, front, work, twin):
    kids, order = fronts.shape[0], fronts.shape[1]
    tiles = order // TILE
    pivots = S1 // TILE

    def convert(k, _):
        for a in range(tiles):
            rows = slice(a * TILE, (a + 1) * TILE)
            front[k, rows, a * TILE :] = fronts[k, rows, a * TILE :].astype(F32)
        return 0

    lax.fori_loop(0, kids, convert, 0)

    def step(p, _):
        for q in range(pivots):

            @pl.when(p == q)
            def _():
                here = slice(q * TILE, (q + 1) * TILE)
                for k in range(kids):
                    load_tile(work, twin, kids, k, front[k, here, here])

        factor_tiles(work, twin, kids)
        for q in range(pivots):

            @pl.when(p == q)
            def _():
                here = slice(q * TILE, (q + 1) * TILE)
                edge = (q + 1) * TILE

                def apply(k, _):
                    inverse = work[pl.ds((kids + k) * TILE, TILE), :]
                    x = dot_nn(inverse, front[k, here, edge:])
                    xt = x.T
                    lower[k, :, here] = xt[S1 - edge :, :].astype(jnp.bfloat16)
                    th, tl = split(xt)
                    xh, xl = split(x)
                    left = jnp.concatenate([th, th, tl], axis=1)
                    right = jnp.concatenate([xh, xl, xh], axis=0)
                    for a in range(q + 1, tiles):
                        rows = slice(a * TILE, (a + 1) * TILE)
                        off = (a - q - 1) * TILE
                        fresh = front[k, rows, a * TILE :] - jnp.dot(
                            left[off : off + TILE, :], right[:, off:], preferred_element_type=F32
                        )
                        if q < pivots - 1:
                            front[k, rows, a * TILE :] = fresh
                        elif a == pivots:
                            outgoing[target[k], :TILE, :] = fresh[:, :TILE]
                            outgoing[target[k], TILE : 2 * TILE, :] = fresh[:, TILE:]
                        else:
                            outgoing[target[k], 2 * TILE :, :] = fresh
                    return 0

                lax.fori_loop(0, kids, apply, 0)

        return 0

    lax.fori_loop(0, pivots, step, 0)


def tile_number(a, b):
    return a * PT - a * (a - 1) // 2 + (b - a)


def gather_kernel(tiles, slots, parent, dense):
    dense[...] = jnp.zeros_like(dense)
    band = parent.shape[0] // TILE
    first = lax.axis_index("row") * band
    for n in range(band):
        for b in range(PT):

            @pl.when(b >= first + n)
            def _():
                dense[tile_number(first + n, b)] = parent[
                    n * TILE : (n + 1) * TILE, b * TILE : (b + 1) * TILE
                ]

    def add(s, _):
        t0 = tiles[s, 0]
        t1 = tiles[s, 1]

        @pl.when(t1 > 0)
        def _():
            for m, (a, b) in enumerate(((t0, t0), (t0, t1), (t1, t1))):
                n = tile_number(a, b)
                dense[n] = dense[n] + slots[s, m * TILE : (m + 1) * TILE, :]

        return 0

    lax.fori_loop(0, slots.shape[0], add, 0)


def parent_kernel(dense, panel, rest, front, column, work, twin):
    height = panel.shape[0]
    split_row = PT2 * TILE
    for a in range(PT):
        for b in range(a, PT):
            tile = dense[tile_number(a, b)]
            front[a * TILE : (a + 1) * TILE, b * TILE : (b + 1) * TILE] = tile
            if PT2 <= a < b:
                front[b * TILE : (b + 1) * TILE, a * TILE : (a + 1) * TILE] = tile.T
    column[...] = jnp.zeros_like(column)
    r = lax.broadcasted_iota(jnp.int32, (TILE, TILE), 0)
    c = lax.broadcasted_iota(jnp.int32, (TILE, TILE), 1)

    def step(p, _):
        for q in range(PT2):

            @pl.when(p == q)
            def _():
                here = slice(q * TILE, (q + 1) * TILE)
                load_tile(work, twin, 1, 0, front[here, here])

        factor_tiles(work, twin, 1)
        for q in range(PT2):

            @pl.when(p == q)
            def _():
                here = slice(q * TILE, (q + 1) * TILE)
                edge = (q + 1) * TILE
                column[here, here] = jnp.where(r >= c, work[:TILE, :].T, 0.0)
                x = dot_nn(work[TILE:, :], front[here, edge:])
                xt = x.T
                column[edge:, here] = xt
                th, tl = split(xt)
                xh, xl = split(x)
                left = jnp.concatenate([th, th, tl], axis=1)
                right = jnp.concatenate([xh, xl, xh], axis=0)
                for a in range(q + 1, PT):
                    rows = slice(a * TILE, (a + 1) * TILE)
                    start = min(a, PT2) * TILE
                    off = a * TILE - edge
                    front[rows, start:] = front[rows, start:] - jnp.dot(
                        left[off : off + TILE, :],
                        right[:, start - edge :],
                        preferred_element_type=F32,
                    )

        return 0

    lax.fori_loop(0, PT2, step, 0)
    first = pl.multiple_of(lax.axis_index("row") * height, TILE)
    panel[...] = column[pl.ds(first, height), :]

    @pl.when(first >= split_row)
    def _():
        rest[...] = front[pl.ds(first, height), split_row:]

    @pl.when(first < split_row)
    def _():
        rest[...] = jnp.zeros_like(rest)


def params():
    return pltpu.CompilerParams(vmem_limit_bytes=VMEM_BYTES)


VM = pl.BlockSpec(memory_space=pltpu.VMEM)
SM = pl.BlockSpec(memory_space=pltpu.SMEM)


def run_children(fronts, target, slots):
    kids, order, _ = fronts.shape
    return pl.pallas_call(
        child_kernel,
        in_specs=[SM, VM],
        out_specs=[VM, VM],
        out_shape=[
            jax.ShapeDtypeStruct((kids, order - S1, S1), jnp.bfloat16),
            jax.ShapeDtypeStruct((slots, 3 * TILE, TILE), F32),
        ],
        scratch_shapes=[
            pltpu.VMEM((kids, order, order), F32),
            pltpu.VMEM((2 * kids * TILE, TILE), F32),
            pltpu.VMEM((2 * kids * TILE, TILE), F32),
        ],
        compiler_params=params(),
        name="children",
    )(target, fronts)


def run_gather(tiles, slots, parent):
    return pl.pallas_call(
        gather_kernel,
        in_specs=[SM, VM, VM],
        out_specs=VM,
        out_shape=jax.ShapeDtypeStruct((PT * (PT + 1) // 2, TILE, TILE), F32),
        compiler_params=params(),
        name="assemble",
    )(tiles, slots, parent)


def run_parent(dense, height):
    return pl.pallas_call(
        parent_kernel,
        in_specs=[VM],
        out_specs=[VM, VM],
        out_shape=[
            jax.ShapeDtypeStruct((height, PT2 * TILE), F32),
            jax.ShapeDtypeStruct((height, (PT - PT2) * TILE), F32),
        ],
        scratch_shapes=[
            pltpu.VMEM((PT * TILE, PT * TILE), F32),
            pltpu.VMEM((PT * TILE, PT2 * TILE), F32),
            pltpu.VMEM((2 * TILE, TILE), F32),
            pltpu.VMEM((2 * TILE, TILE), F32),
        ],
        compiler_params=params(),
        name="parent",
    )(dense)


def local(child_fronts, child_tiles, child_parent, parent_front):
    groups = lax.axis_size("col")
    kid_count = child_parent.shape[0]
    parent_ids = child_parent[:, 0]
    kid_order = jnp.arange(kid_count)
    earlier = (parent_ids[:, None] == parent_ids[None, :]) & (
        kid_order[None, :] < kid_order[:, None]
    )
    slot_index = jnp.sum(earlier.astype(jnp.int32), axis=1)
    target = parent_ids * CAP + slot_index
    chosen = target[None, :] == jnp.arange(groups * CAP)[:, None]
    outgoing_tiles = jnp.sum(
        jnp.where(chosen[:, :, None], child_tiles[None, :, :], 0), axis=1
    ).astype(jnp.int32)
    child_lower, outgoing = run_children(child_fronts, target, groups * CAP)
    received = lax.all_to_all(outgoing, "col", split_axis=0, concat_axis=0, tiled=True)
    received_tiles = lax.all_to_all(
        outgoing_tiles, "col", split_axis=0, concat_axis=0, tiled=True
    )
    dense = run_gather(received_tiles, received, parent_front[0])
    dense = lax.psum(dense, "row")
    parent_panel, parent_rest = run_parent(dense, parent_front.shape[1])
    return (child_lower, parent_panel[None], parent_rest[None])


def solution(mesh):
    placed = (
        P(("row", "col"), None, None),
        P(("row", "col"), None),
        P(("row", "col"), None),
        P("col", "row", None),
    )
    return jax.shard_map(
        local,
        mesh=mesh,
        in_specs=placed,
        out_specs=(P(("row", "col"), None, None), P("col", "row", None), P("col", "row", None)),
        check_vma=False,
    )
```

time: 1040 us -> 220 us (0.21)
  other arithmetic: 607 us -> 2.41 us
  waiting for transfers between devices: 260 us -> 124 us
  local copies, waits for them, and re-layouts: 76.4 us -> 3.07 us
  Pallas kernels: 0 us -> 62.4 us
  matrix products: 35.2 us -> 0 us
  blocking collectives: 26.5 us -> 0 us
    another operation x40 -> x0, other arithmetic: 574 us -> none  [the longest x16 318 us: factor_children(): lower_factors = jnp.linalg.cholesky(pivot_blocks)]
    psum x4 -> x1, waiting for transfers between devices: 125 us -> 54.8 us  [local(): dense = lax.psum(dense, 'row')]
    pallas_call x0 -> x3, Pallas kernels: none -> 62.4 us  [the longest x1 34.1 us: run_children(): pl.pallas_call(child_kernel, in_specs=[SM, VM], out_specs=[VM, VM], out_s...]
    reduce_scatter x1 -> x0, waiting for transfers between devices: 42.3 us -> none  [local(): lax.psum_scatter(summed_front, 'row', scatter_dimension=0, tiled=True)]
    all_gather x4 -> x0, blocking collectives: 26.5 us -> none  [local(): column = lax.all_gather(own_rows, 'row', axis=0, tiled=True)]
    another operation x17 -> x0, matrix products: 26.2 us -> none  [the longest x6 14.7 us: factor_children(): lower_factors = jnp.linalg.cholesky(pivot_blocks)]
    all_to_all x1, waiting for transfers between devices: 92.3 us -> 69.4 us  [local(): lax.all_to_all(outgoing, 'col', split_axis=0, concat_axis=0, tiled=True)]
    another operation x18 -> x0, local copies, waits for them, and re-layouts: 19.3 us -> none
  transfers between devices with their start and end apart: 7 -> 3, of which waited for: 6 -> 2; matrix products, arithmetic and copies ran while one was open for 55% -> 0% of each run, Pallas kernels for 0% -> 16%
where the time goes in v1:
time: 220 us; the launch traced here: 219 us
  waiting for transfers between devices  124 us (56%)
  Pallas kernels  62.4 us (28%)
  between operations  14 us (6%)
  starting transfers between devices  13.3 us (6%)
  local copies, waits for them, and re-layouts  3.07 us (1%)
  other arithmetic  2.41 us (1%)
    all_to_all x1, waiting for transfers between devices, local(): lax.all_to_all(outgoing, 'col', split_axis=0, concat_axis=0, tiled=True)  69.4 us
    psum x1, waiting for transfers between devices, local(): dense = lax.psum(dense, 'row')  54.8 us
    pallas_call x1, Pallas kernels, run_children(): pl.pallas_call(child_kernel, in_specs=[SM, VM], out_specs=[VM, VM], out_s...  34.1 us
    pallas_call x1, Pallas kernels, run_parent(): pl.pallas_call(parent_kernel, in_specs=[VM], out_specs=[VM, VM], out_shap...  23.8 us
    all_to_all x1, starting transfers between devices, local(): lax.all_to_all(outgoing_tiles, 'col', split_axis=0, concat_axis=0, tiled=...  7.25 us
    all_to_all x1, starting transfers between devices, local(): lax.all_to_all(outgoing, 'col', split_axis=0, concat_axis=0, tiled=True)  5.99 us
    pallas_call x1, Pallas kernels, run_gather(): pl.pallas_call(gather_kernel, in_specs=[SM, VM, VM], out_specs=VM, out_sh...  4.49 us
  transfers between devices with their start and end apart: 3, of which 2 were waited for; matrix products, arithmetic and copies ran while one was open for 0% of the time, Pallas kernels for 16%

profile of v1, /device:TPU:0, one launch (start us, length us, event | category | flops | bytes accessed | tf_op | source)
XLA Modules:
  0.0 219.5 jit_solution(13520928722940591913)
XLA Ops:
  7.2 0.9 convert_reduce_fusion
  8.1 0.7 multiply_add_fusion.target
  8.7 0.0 copy-start.1
  8.7 0.1 iota_compare_fusion
  8.8 0.8 select_reduce_fusion
  9.6 0.1 all_to_all.10
  9.7 0.6 copy.15
  10.3 7.3 %all-to-all-start = ((s32[8,2,2]{1,2,0:T(2,128)}), s32[8,2,2]{1,2,0:T(2,128)S(1)}, u32[]{:S(2)}, u32[]{:S(2)}) async-start(s32[8,2,2]{1,2,0:T(2,128)} %copy.15), calls=%async_computation | async-start | bytes 16384 | tf_op jit(solution)/shard_map/all_to_all | solution.py:322
  17.5 0.0 copy-done.1
  17.5 34.1 %children.1 = (bf16[4,256,512]{2,1,0:T(8,128)(2,1)}, f32[16,384,128]{2,1,0:T(8,128)}) custom-call(s32[4]{0:T(128)} %copy-done.1, bf16[4,768,768]{2,1,0:T(8,128)(2,1)} %fronts.1), custom_call_target="tpu_custom_call" | custom-call | tf_op jit(solution)/shard_map/children/pallas_call | solution.py:257
  51.6 0.0 all-to-all-done
  51.6 6.0 %all-to-all-start.1 = ((f32[16,384,128]{2,1,0:T(8,128)}), f32[16,384,128]{2,1,0:T(8,128)S(1)}, u32[]{:S(2)}, u32[]{:S(2)}) async-start(f32[16,384,128]{2,1,0:T(8,128)} %get-tuple-element.8), calls=%async_computation.1 | async-start | bytes 6291456 | tf_op jit(solution)/shard_map/all_to_all | solution.py:321
  57.6 0.0 all-reduce.2.cloned.1.call-start
  57.7 0.7 copy.18
  58.4 69.4 %all-to-all-done.1.slots = f32[16,384,128]{2,1,0:T(8,128)S(1)} async-done(((f32[16,384,128]{2,1,0:T(8,128)}), f32[16,384,128]{2,1,0:T(8,128)S(1)}, u32[]{:S(2)}, u32[]{:S(2)}) %all-to-all-start.1) | async-done | bytes 3145760 | tf_op jit(solution)/shard_map/all_to_all | solution.py:321
  127.8 0.0 copy-start
  127.8 1.6 copy-done
  129.4 4.5 %assemble.1 = f32[36,128,128]{2,1,0:T(8,128)} custom-call(s32[16,2]{1,0:T(8,128)} %bitcast.9, f32[16,384,128]{2,1,0:T(8,128)} %copy-done, f32[256,1024]{1,0:T(8,128)} %bitcast.8), custom_call_target="tpu_custom_call" | custom-call | tf_op jit(solution)/shard_map/assemble/pallas_call | solution.py:276
  133.9 0.0 all-reduce.2.cloned.1.call-update
  133.9 54.8 %all-reduce.2.cloned.1.call-done.dense = f32[36,128,128]{2,1,0:T(8,128)} async-done(((f32[36,128,128]{2,1,0:T(8,128)}), f32[36,128,128]{2,1,0:T(8,128)}) %all-reduce.2.cloned.1.call-update) | async-done | bytes 2359312 | tf_op jit(solution)/shard_map/psum | solution.py:326
  188.8 23.8 %parent.1 = (f32[256,512]{1,0:T(8,128)}, f32[256,512]{1,0:T(8,128)}) custom-call(f32[36,128,128]{2,1,0:T(8,128)} %all-reduce.2.cloned.1.call-done.dense), custom_call_target="tpu_custom_call" | custom-call | tf_op jit(solution)/shard_map/parent/pallas_call | solution.py:287
Async XLA Ops:
  8.7 8.8 %copy-start.1 = (s32[4]{0:T(128)}, s32[4]{0:T(128)S(1)}, u32[]{:S(2)}) copy-start(s32[4]{0:T(128)S(1)} %multiply_add_fusion.target) | copy-start | bytes 52
  10.3 41.4 %all-to-all-start = ((s32[8,2,2]{1,2,0:T(2,128)}), s32[8,2,2]{1,2,0:T(2,128)S(1)}, u32[]{:S(2)}, u32[]{:S(2)}) async-start(s32[8,2,2]{1,2,0:T(2,128)} %copy.15), calls=%async_computation | async-start | bytes 16384 | tf_op jit(solution)/shard_map/all_to_all | solution.py:322
  51.6 76.1 %all-to-all-start.1 = ((f32[16,384,128]{2,1,0:T(8,128)}), f32[16,384,128]{2,1,0:T(8,128)S(1)}, u32[]{:S(2)}, u32[]{:S(2)}) async-start(f32[16,384,128]{2,1,0:T(8,128)} %get-tuple-element.8), calls=%async_computation.1 | async-start | bytes 6291456 | tf_op jit(solution)/shard_map/all_to_all | solution.py:321
  57.6 131.1 %all-reduce.2.cloned.1.call-start = ((), (), s32[]{:S(2)}) async-start(), calls=%async_computation.2 | async-start | bytes 4718592 | tf_op jit(solution)/shard_map/psum | solution.py:326
  127.8 1.7 copy-start
Sparse Core Ops, SparseCore 0:
  134.1 54.6 all-reduce.1

commit v2 on v1

--- a/solution.py
+++ b/solution.py
@@ -13,6 +13,9 @@
 PT2 = 4
 CAP = 2
 STRIP = 16
+EXTRA = 8
+PIVOT_TILES = PT2 * (PT2 + 1) // 2
+ALL_TILES = PT * (PT + 1) // 2
 VMEM_BYTES = 56 * 1024 * 1024
 F32 = jnp.float32
 
@@ -90,10 +93,13 @@
     work[mirror, :] = jnp.where(r == c, 1.0, 0.0).astype(F32)
 
 
-def child_kernel(target, fronts, lower, outgoing, front, work, twin):
+def child_kernel(parents, places, fronts, lower, outgoing, front, work, twin):
     kids, order = fronts.shape[0], fronts.shape[1]
     tiles = order // TILE
     pivots = S1 // TILE
+    row = lax.broadcasted_iota(jnp.int32, (TILE, TILE), 0)
+    lane = lax.broadcasted_iota(jnp.int32, (TILE, TILE), 1)
+    outgoing[:, 2 * TILE :, :] = jnp.zeros((outgoing.shape[0], EXTRA, TILE), F32)
 
     def convert(k, _):
         for a in range(tiles):
@@ -102,6 +108,21 @@
         return 0
 
     lax.fori_loop(0, kids, convert, 0)
+
+    def send(k, top, corner):
+        slot = parents[k, 0] * CAP
+        for other in range(kids):
+            same = (parents[other, 0] == parents[k, 0]) & (other < k)
+            slot = slot + same.astype(jnp.int32)
+        outgoing[slot, :TILE, :] = top[:, TILE:]
+        outgoing[slot, TILE : 2 * TILE, :] = jnp.where(row <= lane, top[:, :TILE], corner)
+        diagonal = jnp.sum(jnp.where(row == lane, corner, 0.0), axis=0, keepdims=True)
+        r = row[:EXTRA]
+        c = lane[:EXTRA]
+        ids = jnp.where(c == 0, places[k, 0], places[k, 1]).astype(F32)
+        outgoing[slot, 2 * TILE :, :] = jnp.where(
+            r == 0, jnp.broadcast_to(diagonal, (EXTRA, TILE)), ids
+        )
 
     def step(p, _):
         for q in range(pivots):
@@ -129,6 +150,7 @@
                     xh, xl = split(x)
                     left = jnp.concatenate([th, th, tl], axis=1)
                     right = jnp.concatenate([xh, xl, xh], axis=0)
+                    last = []
                     for a in range(q + 1, tiles):
                         rows = slice(a * TILE, (a + 1) * TILE)
                         off = (a - q - 1) * TILE
@@ -137,11 +159,10 @@
                         )
                         if q < pivots - 1:
                             front[k, rows, a * TILE :] = fresh
-                        elif a == pivots:
-                            outgoing[target[k], :TILE, :] = fresh[:, :TILE]
-                            outgoing[target[k], TILE : 2 * TILE, :] = fresh[:, TILE:]
                         else:
-                            outgoing[target[k], 2 * TILE :, :] = fresh
+                            last.append(fresh)
+                    if last:
+                        send(k, *last)
                     return 0
 
                 lax.fori_loop(0, kids, apply, 0)
@@ -151,14 +172,28 @@
     lax.fori_loop(0, pivots, step, 0)
 
 
+def corner_number(a, b):
+    return a * PT2 - a * (a - 1) // 2 + (b - a)
+
+
 def tile_number(a, b):
-    return a * PT - a * (a - 1) // 2 + (b - a)
+    if isinstance(a, int) and isinstance(b, int):
+        if b < PT2:
+            return corner_number(a, b)
+        if a < PT2:
+            return PIVOT_TILES + a * PT2 + b - PT2
+        return PIVOT_TILES + PT2 * PT2 + corner_number(a - PT2, b - PT2)
+    beside = PIVOT_TILES + a * PT2 + b - PT2
+    after = PIVOT_TILES + PT2 * PT2 + corner_number(a - PT2, b - PT2)
+    return jnp.where(b < PT2, corner_number(a, b), jnp.where(a < PT2, beside, after))
 
 
 def gather_kernel(tiles, slots, parent, dense):
     dense[...] = jnp.zeros_like(dense)
     band = parent.shape[0] // TILE
     first = lax.axis_index("row") * band
+    row = lax.broadcasted_iota(jnp.int32, (TILE, TILE), 0)
+    lane = lax.broadcasted_iota(jnp.int32, (TILE, TILE), 1)
     for n in range(band):
         for b in range(PT):
 
@@ -174,24 +209,96 @@
 
         @pl.when(t1 > 0)
         def _():
-            for m, (a, b) in enumerate(((t0, t0), (t0, t1), (t1, t1))):
-                n = tile_number(a, b)
-                dense[n] = dense[n] + slots[s, m * TILE : (m + 1) * TILE, :]
+            both = slots[s, TILE : 2 * TILE, :]
+            diagonal = jnp.broadcast_to(slots[s, 2 * TILE : 2 * TILE + 1, :], (TILE, TILE))
+            n = tile_number(t0, t0)
+            dense[n] = dense[n] + jnp.where(row <= lane, both, 0.0)
+            n = tile_number(t0, t1)
+            dense[n] = dense[n] + slots[s, :TILE, :]
+            n = tile_number(t1, t1)
+            mirrored = jnp.where(row < lane, both.T, 0.0)
+            dense[n] = dense[n] + jnp.where(row == lane, diagonal, mirrored)
 
         return 0
 
     lax.fori_loop(0, slots.shape[0], add, 0)
 
 
-def parent_kernel(dense, panel, rest, front, column, work, twin):
+def parent_kernel(
+    ranks, dense, panel, rest, front, column, work, twin, inverses, total, fetched, halves, heard,
+    core_send, core_recv, far_send, far_recv, back_send, back_recv,
+):
     height = panel.shape[0]
-    split_row = PT2 * TILE
-    for a in range(PT):
-        for b in range(a, PT):
-            tile = dense[tile_number(a, b)]
-            front[a * TILE : (a + 1) * TILE, b * TILE : (b + 1) * TILE] = tile
-            if PT2 <= a < b:
-                front[b * TILE : (b + 1) * TILE, a * TILE : (a + 1) * TILE] = tile.T
+    cut = PT2 * TILE
+    me = lax.axis_index("row")
+    core = lax.rem(me, 2)
+    place = lax.div(me, 2)
+    chips = ranks // 2
+    partner = place * 2 + 1 - core
+    peers = [lax.rem(place + d, chips) * 2 + core for d in range(1, chips)]
+    other_half = PT2 * PT2 + PIVOT_TILES
+    parts = ((0, PIVOT_TILES // 2, 0), (PIVOT_TILES, other_half // 2, PIVOT_TILES // 2))
+
+    barrier = pltpu.get_barrier_semaphore()
+    for device in [partner] + peers:
+        pl.semaphore_signal(
+            barrier, inc=1, device_id={"row": device}, device_id_type=pl.DeviceIdType.MESH
+        )
+    pl.semaphore_wait(barrier, chips)
+
+    def copy(source, target, send, recv, device):
+        return pltpu.make_async_remote_copy(
+            src_ref=source,
+            dst_ref=target,
+            send_sem=send,
+            recv_sem=recv,
+            device_id={"row": device},
+            device_id_type=pl.DeviceIdType.MESH,
+        )
+
+    near, far, back = [], [], []
+    for i, (base, n, off) in enumerate(parts):
+        near.append(
+            copy(
+                dense.at[pl.ds(base + (1 - core) * n, n)],
+                fetched.at[pl.ds(off, n)],
+                core_send.at[i],
+                core_recv.at[i],
+                partner,
+            )
+        )
+        near[i].start()
+    for i, (base, n, off) in enumerate(parts):
+        near[i].wait()
+        here = pl.ds(off, n)
+        halves[here] = dense[pl.ds(base + core * n, n)] + fetched[here]
+        far.append(
+            [
+                copy(halves.at[here], heard.at[d, here], far_send.at[i, d], far_recv.at[i, d], peer)
+                for d, peer in enumerate(peers)
+            ]
+        )
+        for one in far[i]:
+            one.start()
+
+    def finish(i):
+        base, n, off = parts[i]
+        mine = pl.ds(base + core * n, n)
+        here = pl.ds(off, n)
+        for one in far[i]:
+            one.wait()
+        value = halves[here]
+        for d in range(len(peers)):
+            value = value + heard[d, here]
+        total[mine] = value
+        back = copy(total.at[mine], total.at[mine], back_send.at[i], back_recv.at[i], partner)
+        back.start()
+        back.wait()
+
+    finish(0)
+    for a in range(PT2):
+        for b in range(a, PT2):
+            front[a * TILE : (a + 1) * TILE, b * TILE : (b + 1) * TILE] = total[tile_number(a, b)]
     column[...] = jnp.zeros_like(column)
     r = lax.broadcasted_iota(jnp.int32, (TILE, TILE), 0)
     c = lax.broadcasted_iota(jnp.int32, (TILE, TILE), 1)
@@ -212,55 +319,65 @@
                 here = slice(q * TILE, (q + 1) * TILE)
                 edge = (q + 1) * TILE
                 column[here, here] = jnp.where(r >= c, work[:TILE, :].T, 0.0)
-                x = dot_nn(work[TILE:, :], front[here, edge:])
+                inverses[q] = work[TILE:, :]
+                if q == PT2 - 1:
+                    return
+                x = dot_nn(work[TILE:, :], front[here, edge:cut])
                 xt = x.T
-                column[edge:, here] = xt
-                th, tl = split(xt)
-                xh, xl = split(x)
-                left = jnp.concatenate([th, th, tl], axis=1)
-                right = jnp.concatenate([xh, xl, xh], axis=0)
-                for a in range(q + 1, PT):
-                    rows = slice(a * TILE, (a + 1) * TILE)
-                    start = min(a, PT2) * TILE
-                    off = a * TILE - edge
-                    front[rows, start:] = front[rows, start:] - jnp.dot(
-                        left[off : off + TILE, :],
-                        right[:, start - edge :],
-                        preferred_element_type=F32,
-                    )
+                column[edge:cut, here] = xt
+                front[edge:cut, edge:cut] = front[edge:cut, edge:cut] - dot_nn(xt, x)
 
         return 0
 
     lax.fori_loop(0, PT2, step, 0)
-    first = pl.multiple_of(lax.axis_index("row") * height, TILE)
+    finish(1)
+    for q in range(PT2):
+        here = slice(q * TILE, (q + 1) * TILE)
+        right = jnp.concatenate([total[tile_number(q, b)] for b in range(PT2, PT)], axis=1)
+        if q:
+            right = right - dot_nn(column[here, : q * TILE], front[: q * TILE, cut:])
+        front[here, cut:] = dot_nn(inverses[q], right)
+    x = front[:cut, cut:]
+    xt = x.T
+    column[cut:, :] = xt
+    for a in range(PT2, PT):
+        for b in range(a, PT):
+            tile = total[tile_number(a, b)]
+            if a == b:
+                tile = jnp.where(r <= c, tile, tile.T)
+            else:
+                front[b * TILE : (b + 1) * TILE, a * TILE : (a + 1) * TILE] = tile.T
+            front[a * TILE : (a + 1) * TILE, b * TILE : (b + 1) * TILE] = tile
+    front[cut:, cut:] = front[cut:, cut:] - dot_nn(xt, x)
+    first = pl.multiple_of(me * height, TILE)
     panel[...] = column[pl.ds(first, height), :]
 
-    @pl.when(first >= split_row)
+    @pl.when(first >= cut)
     def _():
-        rest[...] = front[pl.ds(first, height), split_row:]
-
-    @pl.when(first < split_row)
+        rest[...] = front[pl.ds(first, height), cut:]
+
+    @pl.when(first < cut)
     def _():
         rest[...] = jnp.zeros_like(rest)
 
 
-def params():
-    return pltpu.CompilerParams(vmem_limit_bytes=VMEM_BYTES)
+def params(**more):
+    return pltpu.CompilerParams(vmem_limit_bytes=VMEM_BYTES, **more)
 
 
 VM = pl.BlockSpec(memory_space=pltpu.VMEM)
 SM = pl.BlockSpec(memory_space=pltpu.SMEM)
 
 
-def run_children(fronts, target, slots):
+def run_children(fronts, parents, places, slots):
     kids, order, _ = fronts.shape
     return pl.pallas_call(
         child_kernel,
-        in_specs=[SM, VM],
+        in_specs=[SM, SM, VM],
         out_specs=[VM, VM],
         out_shape=[
             jax.ShapeDtypeStruct((kids, order - S1, S1), jnp.bfloat16),
-            jax.ShapeDtypeStruct((slots, 3 * TILE, TILE), F32),
+            jax.ShapeDtypeStruct((slots, 2 * TILE + EXTRA, TILE), F32),
         ],
         scratch_shapes=[
             pltpu.VMEM((kids, order, order), F32),
@@ -269,7 +386,7 @@
         ],
         compiler_params=params(),
         name="children",
-    )(target, fronts)
+    )(parents, places, fronts)
 
 
 def run_gather(tiles, slots, parent):
@@ -277,15 +394,19 @@
         gather_kernel,
         in_specs=[SM, VM, VM],
         out_specs=VM,
-        out_shape=jax.ShapeDtypeStruct((PT * (PT + 1) // 2, TILE, TILE), F32),
+        out_shape=jax.ShapeDtypeStruct((ALL_TILES, TILE, TILE), F32),
         compiler_params=params(),
         name="assemble",
     )(tiles, slots, parent)
 
 
 def run_parent(dense, height):
+    ranks = lax.axis_size("row")
+    peers = max(1, ranks // 2 - 1)
+    half = ALL_TILES // 2
+    dma = pltpu.SemaphoreType.DMA
     return pl.pallas_call(
-        parent_kernel,
+        functools.partial(parent_kernel, ranks),
         in_specs=[VM],
         out_specs=[VM, VM],
         out_shape=[
@@ -297,33 +418,29 @@
             pltpu.VMEM((PT * TILE, PT2 * TILE), F32),
             pltpu.VMEM((2 * TILE, TILE), F32),
             pltpu.VMEM((2 * TILE, TILE), F32),
+            pltpu.VMEM((PT2, TILE, TILE), F32),
+            pltpu.VMEM((ALL_TILES, TILE, TILE), F32),
+            pltpu.VMEM((half, TILE, TILE), F32),
+            pltpu.VMEM((half, TILE, TILE), F32),
+            pltpu.VMEM((peers, half, TILE, TILE), F32),
+            dma((2,)),
+            dma((2,)),
+            dma((2, peers)),
+            dma((2, peers)),
+            dma((2,)),
+            dma((2,)),
         ],
-        compiler_params=params(),
+        compiler_params=params(collective_id=1, has_side_effects=True),
         name="parent",
     )(dense)
 
 
 def local(child_fronts, child_tiles, child_parent, parent_front):
     groups = lax.axis_size("col")
-    kid_count = child_parent.shape[0]
-    parent_ids = child_parent[:, 0]
-    kid_order = jnp.arange(kid_count)
-    earlier = (parent_ids[:, None] == parent_ids[None, :]) & (
-        kid_order[None, :] < kid_order[:, None]
-    )
-    slot_index = jnp.sum(earlier.astype(jnp.int32), axis=1)
-    target = parent_ids * CAP + slot_index
-    chosen = target[None, :] == jnp.arange(groups * CAP)[:, None]
-    outgoing_tiles = jnp.sum(
-        jnp.where(chosen[:, :, None], child_tiles[None, :, :], 0), axis=1
-    ).astype(jnp.int32)
-    child_lower, outgoing = run_children(child_fronts, target, groups * CAP)
+    child_lower, outgoing = run_children(child_fronts, child_parent, child_tiles, groups * CAP)
     received = lax.all_to_all(outgoing, "col", split_axis=0, concat_axis=0, tiled=True)
-    received_tiles = lax.all_to_all(
-        outgoing_tiles, "col", split_axis=0, concat_axis=0, tiled=True
-    )
+    received_tiles = received[:, 2 * TILE + 1, :RT1].astype(jnp.int32)
     dense = run_gather(received_tiles, received, parent_front[0])
-    dense = lax.psum(dense, "row")
     parent_panel, parent_rest = run_parent(dense, parent_front.shape[1])
     return (child_lower, parent_panel[None], parent_rest[None])
 

time: 220 us -> 144 us (0.65)
  waiting for transfers between devices: 124 us -> 0 us
  blocking collectives: 0 us -> 57.5 us
  Pallas kernels: 62.4 us -> 78.2 us
  between operations: 14 us -> 0.64 us
  starting transfers between devices: 13.3 us -> 0 us
  local copies, waits for them, and re-layouts: 3.07 us -> 7.05 us
    all_to_all x2 -> x0, waiting for transfers between devices: 69.4 us -> none  [the longest x1 69.4 us: local(): lax.all_to_all(outgoing, 'col', split_axis=0, concat_axis=0, tiled=True)]
    all_to_all x0 -> x1, blocking collectives: none -> 57.5 us  [local(): lax.all_to_all(outgoing, 'col', split_axis=0, concat_axis=0, tiled=True)]
    psum x1 -> x0, waiting for transfers between devices: 54.8 us -> none  [local(): dense = lax.psum(dense, 'row')]
    pallas_call x2, Pallas kernels: 58 us -> 73.9 us  [the longest x1 40.1 us: run_parent(): pl.pallas_call(functools.partial(parent_kernel, ranks), in_specs=[VM], ou...]
    all_to_all x2 -> x0, starting transfers between devices: 13.2 us -> none  [the longest x1 7.25 us: local(): lax.all_to_all(outgoing_tiles, 'col', split_axis=0, concat_axis=0, tiled=...]
    unnamed x4 -> x6, local copies, waits for them, and re-layouts: 1.65 us -> 7.05 us
  transfers between devices with their start and end apart: 3 -> 0, of which waited for: 2 -> 0; matrix products, arithmetic and copies ran while one was open for 0% -> 0% of each run, Pallas kernels for 16% -> 0%
where the time goes in v2:
time: 144 us
  Pallas kernels  78.2 us (54%)
  blocking collectives  57.5 us (40%)
  local copies, waits for them, and re-layouts  7.05 us (5%)
    all_to_all x1, blocking collectives, local(): lax.all_to_all(outgoing, 'col', split_axis=0, concat_axis=0, tiled=True)  57.5 us
    pallas_call x1, Pallas kernels, run_parent(): pl.pallas_call(functools.partial(parent_kernel, ranks), in_specs=[VM], ou...  40.1 us
    pallas_call x1, Pallas kernels, run_children(): pl.pallas_call(child_kernel, in_specs=[SM, SM, VM], out_specs=[VM, VM], o...  33.8 us
    unnamed x6, local copies, waits for them, and re-layouts  7.05 us
    pallas_call x1, Pallas kernels, run_gather(): pl.pallas_call(gather_kernel, in_specs=[SM, VM, VM], out_specs=VM, out_sh...  4.28 us

profile of v2, /device:TPU:0, one launch (start us, length us, event | category | flops | bytes accessed | tf_op | source)
XLA Modules:
  0.0 144.1 jit_solution(9533558424037596317)
XLA Ops:
  0.6 1.3 copy.12.places
  2.0 1.3 copy.11.parents
  3.3 33.8 %children.1 = (bf16[4,256,512]{2,1,0:T(8,128)(2,1)}, f32[16,264,128]{2,1,0:T(8,128)}) custom-call(s32[4,1]{1,0:T(4,128)} %copy.11.parents, s32[4,2]{1,0:T(4,128)} %copy.12.places, bf16[4,768,768]{2,1,0:T(8,128)(2,1)} %fronts.1), custom_call_target="tpu_custom_call" | custom-call | tf_op jit(solution)/shard_map/children/pallas_call | solution.py:374
  37.1 57.5 %all_to_all.5.slots = f32[16,264,128]{2,1,0:T(8,128)S(1)} all-to-all(f32[16,264,128]{2,1,0:T(8,128)} %get-tuple-element.8), channel_id=1, replica_groups=mesh['row'=4,'col'=8] {'col'}, dimensions={0} | all-to-all | bytes 4325376 | tf_op jit(solution)/shard_map/all_to_all | solution.py:441
  94.7 0.0 copy-start
  94.7 0.7 slice_convert_fusion
  95.3 0.7 copy-done
  96.0 4.3 %assemble.1.dense = f32[36,128,128]{2,1,0:T(8,128)} custom-call(s32[16,2]{1,0:T(8,128)} %bitcast.7, f32[16,264,128]{2,1,0:T(8,128)} %copy-done, f32[256,1024]{1,0:T(8,128)} %bitcast.4), custom_call_target="tpu_custom_call" | custom-call | tf_op jit(solution)/shard_map/assemble/pallas_call | solution.py:393
  100.3 40.1 %parent.1 = (f32[256,512]{1,0:T(8,128)}, f32[256,512]{1,0:T(8,128)}) custom-call(f32[36,128,128]{2,1,0:T(8,128)} %assemble.1.dense), custom_call_target="tpu_custom_call" | custom-call | tf_op jit(solution)/shard_map/parent/pallas_call | solution.py:408
  140.3 1.9 %copy.18 = f32[1,256,512]{2,1,0:T(8,128)} copy(f32[1,256,512]{2,1,0:T(8,128)} %bitcast.6) | data formatting | bytes 1048576
  142.2 1.9 %copy.19 = f32[1,256,512]{2,1,0:T(8,128)} copy(f32[1,256,512]{2,1,0:T(8,128)} %bitcast.5) | data formatting | bytes 1048576
Async XLA Ops:
  94.7 1.3 copy-start

commit v3 on v2

--- a/solution.py
+++ b/solution.py
@@ -14,6 +14,8 @@
 CAP = 2
 STRIP = 16
 EXTRA = 8
+SLOT = 2 * TILE + EXTRA
+CHUNKS = 3
 PIVOT_TILES = PT2 * (PT2 + 1) // 2
 ALL_TILES = PT * (PT + 1) // 2
 VMEM_BYTES = 56 * 1024 * 1024
@@ -93,13 +95,15 @@
     work[mirror, :] = jnp.where(r == c, 1.0, 0.0).astype(F32)
 
 
-def child_kernel(parents, places, fronts, lower, outgoing, front, work, twin):
+def child_kernel(groups, parents, places, fronts, lower, near, far, front, work, twin):
     kids, order = fronts.shape[0], fronts.shape[1]
     tiles = order // TILE
     pivots = S1 // TILE
     row = lax.broadcasted_iota(jnp.int32, (TILE, TILE), 0)
     lane = lax.broadcasted_iota(jnp.int32, (TILE, TILE), 1)
-    outgoing[:, 2 * TILE :, :] = jnp.zeros((outgoing.shape[0], EXTRA, TILE), F32)
+    near[:, :EXTRA, :] = jnp.zeros((near.shape[0], EXTRA, TILE), F32)
+    half = groups // 2
+    base = lax.div(lax.axis_index("col"), half) * half
 
     def convert(k, _):
         for a in range(tiles):
@@ -114,15 +118,21 @@
         for other in range(kids):
             same = (parents[other, 0] == parents[k, 0]) & (other < k)
             slot = slot + same.astype(jnp.int32)
-        outgoing[slot, :TILE, :] = top[:, TILE:]
-        outgoing[slot, TILE : 2 * TILE, :] = jnp.where(row <= lane, top[:, :TILE], corner)
+        slot = slot - base * CAP
+        inside = (slot >= 0) & (slot < half * CAP)
+        crossed = jnp.where(slot < 0, slot + half * CAP, slot - half * CAP)
+        code = jnp.where(inside, -1, crossed)
         diagonal = jnp.sum(jnp.where(row == lane, corner, 0.0), axis=0, keepdims=True)
         r = row[:EXTRA]
         c = lane[:EXTRA]
-        ids = jnp.where(c == 0, places[k, 0], places[k, 1]).astype(F32)
-        outgoing[slot, 2 * TILE :, :] = jnp.where(
-            r == 0, jnp.broadcast_to(diagonal, (EXTRA, TILE)), ids
-        )
+        ids = jnp.where(c == 0, places[k, 0], jnp.where(c == 1, places[k, 1], code)).astype(F32)
+        far[k, :EXTRA, :] = jnp.where(r == 0, jnp.broadcast_to(diagonal, (EXTRA, TILE)), ids)
+        far[k, EXTRA : EXTRA + TILE, :] = top[:, TILE:]
+        far[k, EXTRA + TILE :, :] = jnp.where(row <= lane, top[:, :TILE], corner)
+
+        @pl.when(inside)
+        def _():
+            near[slot] = far[k]
 
     def step(p, _):
         for q in range(pivots):
@@ -209,12 +219,12 @@
 
         @pl.when(t1 > 0)
         def _():
-            both = slots[s, TILE : 2 * TILE, :]
-            diagonal = jnp.broadcast_to(slots[s, 2 * TILE : 2 * TILE + 1, :], (TILE, TILE))
+            both = slots[s, EXTRA + TILE :, :]
+            diagonal = jnp.broadcast_to(slots[s, 0:1, :], (TILE, TILE))
             n = tile_number(t0, t0)
             dense[n] = dense[n] + jnp.where(row <= lane, both, 0.0)
             n = tile_number(t0, t1)
-            dense[n] = dense[n] + slots[s, :TILE, :]
+            dense[n] = dense[n] + slots[s, EXTRA : EXTRA + TILE, :]
             n = tile_number(t1, t1)
             mirrored = jnp.where(row < lane, both.T, 0.0)
             dense[n] = dense[n] + jnp.where(row == lane, diagonal, mirrored)
@@ -222,6 +232,85 @@
         return 0
 
     lax.fori_loop(0, slots.shape[0], add, 0)
+
+
+def exchange_kernel(
+    groups, near, far, received, arrived, relayed, far_send, far_recv, near_send, near_recv,
+    relay_send, relay_recv,
+):
+    half = groups // 2
+    kids = far.shape[0]
+    me = lax.axis_index("col")
+    spot = lax.rem(me, half)
+    base = me - spot
+    across = lax.rem(me + half, groups)
+    mates = [lax.rem(spot + d, half) for d in range(1, half)]
+    size = SLOT // CHUNKS
+    chunks = [pl.ds(n * size, size) for n in range(CHUNKS)]
+
+    barrier = pltpu.get_barrier_semaphore()
+    for device in [across] + [base + mate for mate in mates]:
+        pl.semaphore_signal(
+            barrier, inc=1, device_id={"col": device}, device_id_type=pl.DeviceIdType.MESH
+        )
+    pl.semaphore_wait(barrier, half)
+
+    def copy(source, target, send, recv, device):
+        one = pltpu.make_async_remote_copy(
+            src_ref=source,
+            dst_ref=target,
+            send_sem=send,
+            recv_sem=recv,
+            device_id={"col": device},
+            device_id_type=pl.DeviceIdType.MESH,
+        )
+        one.start()
+        return one
+
+    crossing = [
+        copy(far.at[:, rows], arrived.at[:, rows], far_send.at[n], far_recv.at[n], across)
+        for n, rows in enumerate(chunks)
+    ]
+    pending = [
+        copy(
+            near.at[pl.ds(mate * CAP, CAP)],
+            received.at[pl.ds((d + 1) * CAP, CAP)],
+            near_send.at[d],
+            near_recv.at[d],
+            base + mate,
+        )
+        for d, mate in enumerate(mates)
+    ]
+    received[:CAP] = near[pl.ds(spot * CAP, CAP)]
+    codes = None
+    for n, rows in enumerate(chunks):
+        crossing[n].wait()
+        if codes is None:
+            codes = [
+                jnp.broadcast_to(arrived[k, 1:2, 2:3], (size, TILE)) for k in range(kids)
+            ]
+
+        def sort(slot, _):
+            value = jnp.zeros((size, TILE), F32)
+            for k in range(kids):
+                value = jnp.where(codes[k] == slot.astype(F32), arrived[k, rows, :], value)
+            relayed[slot, rows, :] = value
+            return 0
+
+        lax.fori_loop(0, half * CAP, sort, 0)
+        for d, mate in enumerate(mates):
+            pending.append(
+                copy(
+                    relayed.at[pl.ds(mate * CAP, CAP), rows],
+                    received.at[pl.ds((half + d + 1) * CAP, CAP), rows],
+                    relay_send.at[n, d],
+                    relay_recv.at[n, d],
+                    base + mate,
+                )
+            )
+        received[half * CAP : (half + 1) * CAP, rows, :] = relayed[pl.ds(spot * CAP, CAP), rows, :]
+    for one in pending:
+        one.wait()
 
 
 def parent_kernel(
@@ -369,15 +458,16 @@
 SM = pl.BlockSpec(memory_space=pltpu.SMEM)
 
 
-def run_children(fronts, parents, places, slots):
+def run_children(fronts, parents, places, groups):
     kids, order, _ = fronts.shape
     return pl.pallas_call(
-        child_kernel,
+        functools.partial(child_kernel, groups),
         in_specs=[SM, SM, VM],
-        out_specs=[VM, VM],
+        out_specs=[VM, VM, VM],
         out_shape=[
             jax.ShapeDtypeStruct((kids, order - S1, S1), jnp.bfloat16),
-            jax.ShapeDtypeStruct((slots, 2 * TILE + EXTRA, TILE), F32),
+            jax.ShapeDtypeStruct((groups // 2 * CAP, SLOT, TILE), F32),
+            jax.ShapeDtypeStruct((kids, SLOT, TILE), F32),
         ],
         scratch_shapes=[
             pltpu.VMEM((kids, order, order), F32),
@@ -387,6 +477,29 @@
         compiler_params=params(),
         name="children",
     )(parents, places, fronts)
+
+
+def run_exchange(near, far, groups):
+    mates = groups // 2 - 1
+    dma = pltpu.SemaphoreType.DMA
+    return pl.pallas_call(
+        functools.partial(exchange_kernel, groups),
+        in_specs=[VM, VM],
+        out_specs=VM,
+        out_shape=jax.ShapeDtypeStruct((groups * CAP, SLOT, TILE), F32),
+        scratch_shapes=[
+            pltpu.VMEM(far.shape, F32),
+            pltpu.VMEM(near.shape, F32),
+            dma((CHUNKS,)),
+            dma((CHUNKS,)),
+            dma((mates,)),
+            dma((mates,)),
+            dma((CHUNKS, mates)),
+            dma((CHUNKS, mates)),
+        ],
+        compiler_params=params(collective_id=2, has_side_effects=True),
+        name="exchange",
+    )(near, far)
 
 
 def run_gather(tiles, slots, parent):
@@ -437,9 +550,9 @@
 
 def local(child_fronts, child_tiles, child_parent, parent_front):
     groups = lax.axis_size("col")
-    child_lower, outgoing = run_children(child_fronts, child_parent, child_tiles, groups * CAP)
-    received = lax.all_to_all(outgoing, "col", split_axis=0, concat_axis=0, tiled=True)
-    received_tiles = received[:, 2 * TILE + 1, :RT1].astype(jnp.int32)
+    child_lower, near, far = run_children(child_fronts, child_parent, child_tiles, groups)
+    received = run_exchange(near, far, groups)
+    received_tiles = received[:, 1, :RT1].astype(jnp.int32)
     dense = run_gather(received_tiles, received, parent_front[0])
     parent_panel, parent_rest = run_parent(dense, parent_front.shape[1])
     return (child_lower, parent_panel[None], parent_rest[None])

time: 144 us -> 131 us (0.910); the launches traced: 144 us -> 129 us
  blocking collectives: 57.5 us -> 0 us
  Pallas kernels: 78.2 us -> 121 us
    all_to_all x1 -> x0, blocking collectives: 57.5 us -> none  [local(): lax.all_to_all(outgoing, 'col', split_axis=0, concat_axis=0, tiled=True)]
    pallas_call x1 -> x2, Pallas kernels: 33.8 us -> 76.5 us  [the longest x1 42.8 us: run_exchange(): pl.pallas_call(functools.partial(exchange_kernel, groups), in_specs=[VM,...]
    unnamed x6 -> x4, local copies, waits for them, and re-layouts: 7.05 us -> 6.38 us
where the time goes in v3:
time: 131 us; the launch traced here: 129 us
  Pallas kernels  121 us (92%)
  local copies, waits for them, and re-layouts  6.38 us (5%)
  other arithmetic  1.45 us (1%)
    pallas_call x1, Pallas kernels, run_exchange(): pl.pallas_call(functools.partial(exchange_kernel, groups), in_specs=[VM,...  42.8 us
    pallas_call x1, Pallas kernels, run_parent(): pl.pallas_call(functools.partial(parent_kernel, ranks), in_specs=[VM], ou...  40.1 us
    pallas_call x1, Pallas kernels, run_children(): pl.pallas_call(functools.partial(child_kernel, groups), in_specs=[SM, SM,...  33.7 us
    unnamed x4, local copies, waits for them, and re-layouts  6.38 us
    pallas_call x1, Pallas kernels, run_gather(): pl.pallas_call(gather_kernel, in_specs=[SM, VM, VM], out_specs=VM, out_sh...  4.38 us

profile of v3, /device:TPU:0, one launch (start us, length us, event | category | flops | bytes accessed | tf_op | source)
XLA Modules:
  0.0 129.4 jit_solution(16454469632874507789)
XLA Ops:
  0.6 1.3 %copy.12.places = s32[4,2]{1,0:T(4,128)} copy(s32[4,2]{0,1:T(2,128)} %param.5) | data formatting | bytes 64 | tf_op args[1]
  2.0 1.3 %copy.11.parents = s32[4,1]{1,0:T(4,128)} copy(s32[4,1]{0,1:T(1,128)} %param.6) | data formatting | bytes 32 | tf_op args[2]
  3.3 33.7 %children.1 = (bf16[4,256,512]{2,1,0:T(8,128)(2,1)}, f32[8,264,128]{2,1,0:T(8,128)}, f32[4,264,128]{2,1,0:T(8,128)}) custom-call(s32[4,1]{1,0:T(4,128)} %copy.11.parents, s32[4,2]{1,0:T(4,128)} %copy.12.places, bf16[4,768,768]{2,1,0:T(8,128)(2,1)} %fronts.1), custom_call_target="tpu_custom_call" | custom-call | tf_op jit(solution)/shard_map/children/pallas_call | solution.py:463
  36.9 42.8 %exchange.1.slots = f32[16,264,128]{2,1,0:T(8,128)} custom-call(f32[8,264,128]{2,1,0:T(8,128)} %get-tuple-element.9.near, f32[4,264,128]{2,1,0:T(8,128)} %get-tuple-element.10.far), custom_call_target="tpu_custom_call" | custom-call | tf_op jit(solution)/shard_map/exchange/pallas_call | solution.py:485
  79.8 1.5 %slice_convert_fusion = s32[16,1,2]{2,1,0:T(1,128)} fusion(f32[16,264,128]{2,1,0:T(8,128)} %exchange.1.slots), kind=kLoop, calls=%fused_computation | loop fusion | flops 32 | bytes 256 | tf_op jit(solution)/shard_map/convert_element_type | solution.py:555
  81.2 4.4 %assemble.1.dense = f32[36,128,128]{2,1,0:T(8,128)} custom-call(s32[16,2]{1,0:T(8,128)} %bitcast.7, f32[16,264,128]{2,1,0:T(8,128)} %exchange.1.slots, f32[256,1024]{1,0:T(8,128)} %bitcast.4), custom_call_target="tpu_custom_call" | custom-call | tf_op jit(solution)/shard_map/assemble/pallas_call | solution.py:506
  85.6 40.1 %parent.1 = (f32[256,512]{1,0:T(8,128)}, f32[256,512]{1,0:T(8,128)}) custom-call(f32[36,128,128]{2,1,0:T(8,128)} %assemble.1.dense), custom_call_target="tpu_custom_call" | custom-call | tf_op jit(solution)/shard_map/parent/pallas_call | solution.py:521
  125.7 1.9 %copy.18 = f32[1,256,512]{2,1,0:T(8,128)} copy(f32[1,256,512]{2,1,0:T(8,128)} %bitcast.6) | data formatting | bytes 1048576
  127.5 1.9 %copy.19 = f32[1,256,512]{2,1,0:T(8,128)} copy(f32[1,256,512]{2,1,0:T(8,128)} %bitcast.5) | data formatting | bytes 1048576

commit v4 on v3

--- a/solution.py
+++ b/solution.py
@@ -95,7 +95,15 @@
     work[mirror, :] = jnp.where(r == c, 1.0, 0.0).astype(F32)
 
 
-def child_kernel(groups, parents, places, fronts, lower, near, far, front, work, twin):
+def child_kernel(
+    groups, parents_far, places_far, fronts, lower, near, far, front, work, twin, parents, places, loads
+):
+    fetches = [
+        pltpu.make_async_copy(parents_far, parents, loads.at[0]),
+        pltpu.make_async_copy(places_far, places, loads.at[1]),
+    ]
+    for one in fetches:
+        one.start()
     kids, order = fronts.shape[0], fronts.shape[1]
     tiles = order // TILE
     pivots = S1 // TILE
@@ -105,13 +113,10 @@
     half = groups // 2
     base = lax.div(lax.axis_index("col"), half) * half
 
-    def convert(k, _):
-        for a in range(tiles):
-            rows = slice(a * TILE, (a + 1) * TILE)
-            front[k, rows, a * TILE :] = fronts[k, rows, a * TILE :].astype(F32)
-        return 0
-
-    lax.fori_loop(0, kids, convert, 0)
+    def read(q, k, rows, lanes):
+        if q == 0:
+            return fronts[k, rows, lanes].astype(F32)
+        return front[k, rows, lanes]
 
     def send(k, top, corner):
         slot = parents[k, 0] * CAP
@@ -141,7 +146,7 @@
             def _():
                 here = slice(q * TILE, (q + 1) * TILE)
                 for k in range(kids):
-                    load_tile(work, twin, kids, k, front[k, here, here])
+                    load_tile(work, twin, kids, k, read(q, k, here, here))
 
         factor_tiles(work, twin, kids)
         for q in range(pivots):
@@ -151,9 +156,13 @@
                 here = slice(q * TILE, (q + 1) * TILE)
                 edge = (q + 1) * TILE
 
+                if q == pivots - 1:
+                    for one in fetches:
+                        one.wait()
+
                 def apply(k, _):
                     inverse = work[pl.ds((kids + k) * TILE, TILE), :]
-                    x = dot_nn(inverse, front[k, here, edge:])
+                    x = dot_nn(inverse, read(q, k, here, slice(edge, order)))
                     xt = x.T
                     lower[k, :, here] = xt[S1 - edge :, :].astype(jnp.bfloat16)
                     th, tl = split(xt)
@@ -164,7 +173,7 @@
                     for a in range(q + 1, tiles):
                         rows = slice(a * TILE, (a + 1) * TILE)
                         off = (a - q - 1) * TILE
-                        fresh = front[k, rows, a * TILE :] - jnp.dot(
+                        fresh = read(q, k, rows, slice(a * TILE, order)) - jnp.dot(
                             left[off : off + TILE, :], right[:, off:], preferred_element_type=F32
                         )
                         if q < pivots - 1:
@@ -462,7 +471,7 @@
     kids, order, _ = fronts.shape
     return pl.pallas_call(
         functools.partial(child_kernel, groups),
-        in_specs=[SM, SM, VM],
+        in_specs=[pl.BlockSpec(memory_space=pl.ANY), pl.BlockSpec(memory_space=pl.ANY), VM],
         out_specs=[VM, VM, VM],
         out_shape=[
             jax.ShapeDtypeStruct((kids, order - S1, S1), jnp.bfloat16),
@@ -473,6 +482,9 @@
             pltpu.VMEM((kids, order, order), F32),
             pltpu.VMEM((2 * kids * TILE, TILE), F32),
             pltpu.VMEM((2 * kids * TILE, TILE), F32),
+            pltpu.SMEM(parents.shape, jnp.int32),
+            pltpu.SMEM(places.shape, jnp.int32),
+            pltpu.SemaphoreType.DMA((2,)),
         ],
         compiler_params=params(),
         name="children",

time: 131 us -> 131 us (level)
  no operation moved by 1% of the time
where the time goes in v4:
time: 131 us; the launch traced here: 129 us
  Pallas kernels  121 us (92%)
  local copies, waits for them, and re-layouts  6.38 us (5%)
  other arithmetic  1.45 us (1%)
    pallas_call x1, Pallas kernels, run_exchange(): pl.pallas_call(functools.partial(exchange_kernel, groups), in_specs=[VM,...  42.9 us
    pallas_call x1, Pallas kernels, run_parent(): pl.pallas_call(functools.partial(parent_kernel, ranks), in_specs=[VM], ou...  40.1 us
    pallas_call x1, Pallas kernels, run_children(): pl.pallas_call(functools.partial(child_kernel, groups), in_specs=[pl.Bloc...  33.3 us
    unnamed x4, local copies, waits for them, and re-layouts  6.38 us
    pallas_call x1, Pallas kernels, run_gather(): pl.pallas_call(gather_kernel, in_specs=[SM, VM, VM], out_specs=VM, out_sh...  4.48 us

profile of v4, /device:TPU:0, one launch (start us, length us, event | category | flops | bytes accessed | tf_op | source)
XLA Modules:
  0.0 129.2 jit_solution(3483482413211302985)
XLA Ops:
  0.6 1.3 %copy.12.places_far = s32[4,2]{1,0:T(4,128)} copy(s32[4,2]{0,1:T(2,128)} %param.5) | data formatting | bytes 64 | tf_op args[1]
  2.0 1.3 %copy.11.parents_far = s32[4,1]{1,0:T(4,128)} copy(s32[4,1]{0,1:T(1,128)} %param.6) | data formatting | bytes 32 | tf_op args[2]
  3.3 33.3 %children.1 = (bf16[4,256,512]{2,1,0:T(8,128)(2,1)}, f32[8,264,128]{2,1,0:T(8,128)}, f32[4,264,128]{2,1,0:T(8,128)}) custom-call(s32[4,1]{1,0:T(4,128)} %copy.11.parents_far, s32[4,2]{1,0:T(4,128)} %copy.12.places_far, bf16[4,768,768]{2,1,0:T(8,128)(2,1)} %fronts.1), custom_call_target="tpu_custom_call" | custom-call | tf_op jit(solution)/shard_map/children/pallas_call | solution.py:472
  36.6 42.9 %exchange.1.slots = f32[16,264,128]{2,1,0:T(8,128)} custom-call(f32[8,264,128]{2,1,0:T(8,128)} %get-tuple-element.9.near, f32[4,264,128]{2,1,0:T(8,128)} %get-tuple-element.10.far), custom_call_target="tpu_custom_call" | custom-call | tf_op jit(solution)/shard_map/exchange/pallas_call | solution.py:497
  79.5 1.5 %slice_convert_fusion = s32[16,1,2]{2,1,0:T(1,128)} fusion(f32[16,264,128]{2,1,0:T(8,128)} %exchange.1.slots), kind=kLoop, calls=%fused_computation | loop fusion | flops 32 | bytes 256 | tf_op jit(solution)/shard_map/convert_element_type | solution.py:567
  80.9 4.5 %assemble.1.dense = f32[36,128,128]{2,1,0:T(8,128)} custom-call(s32[16,2]{1,0:T(8,128)} %bitcast.7, f32[16,264,128]{2,1,0:T(8,128)} %exchange.1.slots, f32[256,1024]{1,0:T(8,128)} %bitcast.4), custom_call_target="tpu_custom_call" | custom-call | tf_op jit(solution)/shard_map/assemble/pallas_call | solution.py:518
  85.4 40.1 %parent.1 = (f32[256,512]{1,0:T(8,128)}, f32[256,512]{1,0:T(8,128)}) custom-call(f32[36,128,128]{2,1,0:T(8,128)} %assemble.1.dense), custom_call_target="tpu_custom_call" | custom-call | tf_op jit(solution)/shard_map/parent/pallas_call | solution.py:533
  125.5 1.9 %copy.18 = f32[1,256,512]{2,1,0:T(8,128)} copy(f32[1,256,512]{2,1,0:T(8,128)} %bitcast.6) | data formatting | bytes 1048576
  127.3 1.9 %copy.19 = f32[1,256,512]{2,1,0:T(8,128)} copy(f32[1,256,512]{2,1,0:T(8,128)} %bitcast.5) | data formatting | bytes 1048576
